TPU v7x, 32 devices: a whole 2x2x4 slice. The times are simulated.
32 devices in a mesh: ctx: 8 (over z, x), dp: 4 (over y, core).
Axes of the slice: x: 2, y: 2, z: 4, core: 2. Of those that a mesh axis runs over, the one named last changes fastest.
Arguments:
- query: bfloat16 [4, 2048, 512], P('dp', 'ctx'), may hold values from -170 to 170
- key: bfloat16 [4, 2048, 128], P('dp', 'ctx'), may hold values from -6.1 to 6.1
- value: bfloat16 [4, 2048, 128], P('dp', 'ctx'), may hold values from -6 to 6
- out_grad: bfloat16 [4, 2048, 512], P('dp', 'ctx'), may hold values from -6 to 6
- output: bfloat16 [4, 2048, 512], P('dp', 'ctx'), may hold values from -6 to 6
- inputs: bfloat16 [4, 2048, 8192], P('dp', 'ctx'), may hold values from -6 to 6
- span_ids: int32 [16], P('ctx'), may hold values from 0 to 15, each once
Outputs:
- query_grad: bfloat16 [4, 2048, 512], P('dp', 'ctx')
- key_grad: bfloat16 [4, 2048, 128], P('dp', 'ctx')
- value_grad: bfloat16 [4, 2048, 128], P('dp', 'ctx')
- grad_weights: float32 [8192, 256], replicated
All inputs are finite; a program needn't handle non-finite values.
Results may differ from a plain program's by a relative error of at most 0.0054.
Values may be sent and summed in bfloat16 or wider, within the bound.
A program may use at most 64 MiB of HBM per device.

v0:
```python
from functools import partial

import jax
import jax.numpy as jnp
from jax import lax
from jax.sharding import PartitionSpec as P

NEG_FILL = -1e30


def from_behind(value, axis, steps):
    count = lax.axis_size(axis)
    pairs = [(source, (source + steps) % count) for source in range(count)]
    return lax.ppermute(value, axis, pairs)


def stats_tile(queries_c, query_block, keys_c, key_block, score_scale, old_max, old_sum):
    block_len = keys_c.shape[0]
    offsets = jnp.arange(block_len, dtype=jnp.int32)
    visible = (key_block * block_len + offsets)[None, None, :] <= (
        query_block * block_len + offsets
    )[None, :, None]
    scores = (
        jnp.einsum("rhe,ke->hrk", queries_c, keys_c, preferred_element_type=jnp.float32)
        * score_scale
    )
    scores = jnp.where(visible, scores, NEG_FILL)
    new_max = jnp.maximum(old_max, jnp.max(scores, axis=-1))
    fresh_sum = jnp.sum(jnp.where(visible, jnp.exp(scores - new_max[:, :, None]), 0.0), axis=-1)
    return (new_max, old_sum * jnp.exp(old_max - new_max) + fresh_sum)


def stats_update(statistics, queries, query_blocks, keys_c, key_block, score_scale):
    running_max, running_sum = statistics
    max_list = []
    sum_list = []
    for slot_q in range(2):
        old_max = running_max[slot_q]
        old_sum = running_sum[slot_q]
        new_max, new_sum = lax.cond(
            key_block <= query_blocks[slot_q],
            partial(
                stats_tile,
                queries[slot_q],
                query_blocks[slot_q],
                keys_c,
                key_block,
                score_scale,
                old_max,
                old_sum,
            ),
            lambda: (old_max, old_sum),
        )
        max_list.append(new_max)
        sum_list.append(new_sum)
    return (jnp.stack(max_list), jnp.stack(sum_list))


def tile_terms(
    queries_c, grads_c, lse_c, delta_c, query_block, keys_c, values_c, key_block, score_scale
):
    block_len = keys_c.shape[0]
    offsets = jnp.arange(block_len, dtype=jnp.int32)
    visible = (key_block * block_len + offsets)[None, None, :] <= (
        query_block * block_len + offsets
    )[None, :, None]
    scores = (
        jnp.einsum("rhe,ke->hrk", queries_c, keys_c, preferred_element_type=jnp.float32)
        * score_scale
    )
    probabilities = jnp.where(visible, jnp.exp(scores - lse_c[:, :, None]), 0.0)
    prob_grads = jnp.einsum("rhe,ke->hrk", grads_c, values_c, preferred_element_type=jnp.float32)
    score_grads = (probabilities * (prob_grads - delta_c[:, :, None]) * score_scale).astype(
        jnp.bfloat16
    )
    probs_low = probabilities.astype(jnp.bfloat16)
    query_added = jnp.einsum("hrk,ke->rhe", score_grads, keys_c, preferred_element_type=jnp.float32)
    key_added = jnp.einsum(
        "hrk,rhe->ke", score_grads, queries_c, preferred_element_type=jnp.float32
    )
    value_added = jnp.einsum("hrk,rhe->ke", probs_low, grads_c, preferred_element_type=jnp.float32)
    return (query_added, key_added, value_added)


def visit(query_side, query_blocks, keys_c, values_c, key_block, score_scale):
    queries, grads_query, lse_all, delta_all = query_side
    added_list = []
    key_sum = jnp.zeros(keys_c.shape, jnp.float32)
    value_sum = jnp.zeros(keys_c.shape, jnp.float32)
    for slot_q in range(2):

        def nothing():
            return (
                jnp.zeros(queries.shape[1:], jnp.float32),
                jnp.zeros(keys_c.shape, jnp.float32),
                jnp.zeros(keys_c.shape, jnp.float32),
            )

        query_added, key_added, value_added = lax.cond(
            key_block <= query_blocks[slot_q],
            partial(
                tile_terms,
                queries[slot_q],
                grads_query[slot_q],
                lse_all[slot_q],
                delta_all[slot_q],
                query_blocks[slot_q],
                keys_c,
                values_c,
                key_block,
                score_scale,
            ),
            nothing,
        )
        added_list.append(query_added)
        key_sum = key_sum + key_added
        value_sum = value_sum + value_added
    return (jnp.stack(added_list), key_sum, value_sum)


def local(query, key, value, out_grad, output, inputs, span_ids):
    tokens_dev = query.shape[1]
    block_len = tokens_dev // 2
    head_width = key.shape[2]
    head_count = query.shape[2] // head_width
    score_scale = head_width ** (-0.5)
    cycle_size = lax.axis_size("ctx")
    rank_here = lax.axis_index("ctx")
    block_table = lax.all_gather(span_ids, "ctx", axis=0, tiled=True)
    queries = query[0].reshape(2, block_len, head_count, head_width)
    grads_query = out_grad[0].reshape(2, block_len, head_count, head_width)
    product = out_grad[0].astype(jnp.float32) * output[0].astype(jnp.float32)
    delta_all = jnp.transpose(
        product.reshape(2, block_len, head_count, head_width).sum(axis=-1), (0, 2, 1)
    )
    start_stats = (
        jnp.full((2, head_count, block_len), NEG_FILL, jnp.float32),
        jnp.zeros((2, head_count, block_len), jnp.float32),
    )
    shard_rows = lax.all_gather(key, "ctx", axis=1, tiled=True)

    def one_shard(shard_index, stats_now):
        owner_rank = shard_index * tokens_dev // tokens_dev
        keys_here = lax.dynamic_slice_in_dim(
            shard_rows[0], (shard_index * tokens_dev).astype(jnp.int32), tokens_dev, 0
        )
        keys_here = keys_here.reshape(2, block_len, head_width)
        owner_blocks = lax.dynamic_slice_in_dim(block_table, 2 * owner_rank, 2, 0)
        for slot_k in range(2):
            stats_now = stats_update(
                stats_now, queries, span_ids, keys_here[slot_k], owner_blocks[slot_k], score_scale
            )
        return stats_now

    running_max, running_sum = lax.fori_loop(
        0, shard_rows.shape[1] // tokens_dev, one_shard, start_stats
    )
    lse_all = running_max + jnp.log(running_sum)
    query_side = (queries, grads_query, lse_all, delta_all)
    query_start = jnp.zeros((2, block_len, head_count, head_width), jnp.float32)
    key_value = jnp.stack([key[0], value[0]])
    grad_start = jnp.zeros((2, tokens_dev, head_width), jnp.float32)

    def cycle_step(cycle_turn, state_now):
        key_value, grad_acc, query_acc = state_now
        arriving = from_behind(key_value, "ctx", 1)
        source = (rank_here - cycle_turn) % cycle_size
        source_blocks = lax.dynamic_slice_in_dim(block_table, 2 * source, 2, 0)
        keys_all = key_value[0].reshape(2, block_len, head_width)
        values_all = key_value[1].reshape(2, block_len, head_width)
        grad_parts = grad_acc.reshape(2, 2, block_len, head_width)
        key_new = []
        value_new = []
        for slot_k in range(2):
            query_added, key_added, value_added = visit(
                query_side,
                span_ids,
                keys_all[slot_k],
                values_all[slot_k],
                source_blocks[slot_k],
                score_scale,
            )
            query_acc = query_acc + query_added
            key_new.append(grad_parts[0, slot_k] + key_added)
            value_new.append(grad_parts[1, slot_k] + value_added)
        updated = jnp.stack([jnp.concatenate(key_new, axis=0), jnp.concatenate(value_new, axis=0)])
        grad_acc = from_behind(updated, "ctx", 1)
        return (arriving, grad_acc, query_acc)

    leftover, grad_acc, query_acc = lax.fori_loop(
        0, cycle_size, cycle_step, (key_value, grad_start, query_start)
    )
    key_grad = grad_acc[0]
    value_grad = grad_acc[1]
    key_low = key_grad.astype(jnp.bfloat16)
    value_low = value_grad.astype(jnp.bfloat16)
    query_low = query_acc.reshape(tokens_dev, head_count * head_width).astype(jnp.bfloat16)
    grad_pair = jnp.concatenate([key_low, value_low], axis=1)
    partial_weights = lax.dot_general(
        inputs[0], grad_pair, (((0,), (0,)), ((), ())), preferred_element_type=jnp.float32
    )
    grad_weights = lax.psum(partial_weights, ("ctx", "dp"))
    return (query_low[None], key_low[None], value_low[None], grad_weights)


def solution(mesh):
    placed = (
        P("dp", "ctx", None),
        P("dp", "ctx", None),
        P("dp", "ctx", None),
        P("dp", "ctx", None),
        P("dp", "ctx", None),
        P("dp", "ctx", None),
        P("ctx"),
    )
    return jax.shard_map(
        local,
        mesh=mesh,
        in_specs=placed,
        out_specs=(P("dp", "ctx", None), P("dp", "ctx", None), P("dp", "ctx", None), P()),
        check_vma=False,
    )
```

profile of v0, /device:TPU:0, one launch (start us, length us, event | category | flops | bytes accessed | tf_op | source)
XLA Modules:
  0.0 639.2 jit_solution(5404886521067237906)
XLA Ops:
  10.0 13.1 %all-reduce = s32[16]{0:T(128)S(1)} all-reduce(s32[16]{0:T(128)S(1)} %dynamic-update-slice), channel_id=1, replica_groups=mesh['ctx'=8,'dp'=4] {'ctx'}, use_global_device_ids=true, to_apply=%add | all-reduce | flops 16 | bytes 128
  23.1 31.7 %all_gather.7 = bf16[1,2048,128]{2,1,0:T(8,128)(2,1)S(1)} all-gather(bf16[1,256,128]{2,1,0:T(8,128)(2,1)} %param.28), channel_id=1, replica_groups=mesh['ctx'=8,'dp'=4] {'ctx'}, dimensions={1}, use_global_device_ids=true | all-gather | bytes 589824 | tf_op jit(solution)/shard_map/all_gather | solution.py:140
  59.4 127.2 %while.37 = (s32[]{:T(128)}, f32[2,4,128]{2,1,0:T(4,128)S(1)}, f32[2,4,128]{2,1,0:T(4,128)S(1)}, s32[16]{0:T(128)S(1)}, s32[2]{0:T(128)}, /*index=5*/bf16[1,2048...) while((s32[]{:T(128)}, f32[2,4,128]{2,1,0:T(4,128)S(1)}, ...), condition=%wide.region_17.18_spmd, body=%wide.region_0.17_spmd.sunk | while | flops 68754464 | bytes 3752886 | solution.py:155
  60.1 1.4 fusion.117
  67.3 3.6 conditional.20
  70.9 3.5 conditional.22
  75.8 3.7 conditional.21
  81.0 1.4 fusion.117
  90.9 1.4 fusion.117
  100.9 1.4 fusion.117
  108.0 3.6 conditional.20
  113.0 3.7 conditional.21
  118.2 1.4 fusion.117
  125.3 3.6 conditional.20
  130.3 3.7 conditional.21
  142.6 3.6 conditional.20
  156.2 3.6 conditional.20
  161.1 3.7 conditional.21
  173.4 3.6 conditional.20
  178.4 3.7 conditional.23
  182.1 3.7 conditional.21
  186.6 250.5 %while.38 = (s32[]{:T(128)}, bf16[2,256,128]{2,1,0:T(8,128)(2,1)S(1)}, f32[2,256,128]{2,1,0:T(8,128)S(1)}, f32[2,128,4,128]{3,1,2,0:T(8,128)S(1)}, s32[]{:T(128)...) while((s32[]{:T(128)}, ...), condition=%wide.region_28.29_spmd.clone, body=%wide.region_19.28_spmd.clone.sunk | while | flops 338625536 | bytes 16294890 | solution.py:190
  187.3 1.4 fusion.119
  194.1 2.4 conditional.25
  196.5 2.5 conditional.27
  199.0 2.4 conditional.24
  201.7 53.0 %collective-permute-start.1 = (f32[2,256,128]{2,1,0:T(8,128)S(1)}, f32[2,256,128]{2,1,0:T(8,128)S(1)}, u32[]{:S(2)}, u32[]{:S(2)}) collective-permute-start(f32[2,256,128]{2,1,0:T(8,128)S(1)} %pad_maximum_fusion.9), channel_id=1, source_target_pairs={{0,4},{4,8},{8,12},{12,16},{16,20},{20,24},{24,28},{28,0},{1,5},{5... | collective-permute-start | bytes 786440 | tf_op jit(solution)/shard_map/while/body/eval_jaxpr/ppermute | solution.py:14
  255.1 7.3 %collective-permute-done = bf16[2,256,128]{2,1,0:T(8,128)(2,1)S(1)} collective-permute-done((bf16[2,256,128]{2,1,0:T(8,128)(2,1)S(1)}, bf16[2,256,128]{2,1,0:T(8,128)(2,1)S(1)}, u32[]{:S(2)}, u32[]{:S(2)}) %collective-permute-start) | collective-permute-done | bytes 131104 | tf_op jit(solution)/shard_map/while/body/eval_jaxpr/ppermute | solution.py:14
  263.0 1.4 fusion.119
  269.8 2.4 conditional.25
  272.3 2.5 conditional.27
  274.8 2.4 conditional.26
  277.4 2.5 collective-permute-start.1
  280.3 7.6 %collective-permute-done = bf16[2,256,128]{2,1,0:T(8,128)(2,1)S(1)} collective-permute-done((bf16[2,256,128]{2,1,0:T(8,128)(2,1)S(1)}, bf16[2,256,128]{2,1,0:T(8,128)(2,1)S(1)}, u32[]{:S(2)}, u32[]{:S(2)}) %collective-permute-start) | collective-permute-done | bytes 131104 | tf_op jit(solution)/shard_map/while/body/eval_jaxpr/ppermute | solution.py:14
  288.6 1.4 fusion.119
  295.4 2.4 conditional.25
  297.9 2.5 conditional.27
  300.6 4.6 collective-permute-start.1
  306.5 6.4 %collective-permute-done = bf16[2,256,128]{2,1,0:T(8,128)(2,1)S(1)} collective-permute-done((bf16[2,256,128]{2,1,0:T(8,128)(2,1)S(1)}, bf16[2,256,128]{2,1,0:T(8,128)(2,1)S(1)}, u32[]{:S(2)}, u32[]{:S(2)}) %collective-permute-start) | collective-permute-done | bytes 131104 | tf_op jit(solution)/shard_map/while/body/eval_jaxpr/ppermute | solution.py:14
  313.5 1.4 fusion.119
  320.4 2.4 conditional.25
  323.2 7.3 %collective-permute-start.1 = (f32[2,256,128]{2,1,0:T(8,128)S(1)}, f32[2,256,128]{2,1,0:T(8,128)S(1)}, u32[]{:S(2)}, u32[]{:S(2)}) collective-permute-start(f32[2,256,128]{2,1,0:T(8,128)S(1)} %pad_maximum_fusion.9), channel_id=1, source_target_pairs={{0,4},{4,8},{8,12},{12,16},{16,20},{20,24},{24,28},{28,0},{1,5},{5... | collective-permute-start | bytes 786440 | tf_op jit(solution)/shard_map/while/body/eval_jaxpr/ppermute | solution.py:14
  330.5 1.8 collective-permute-start
  332.6 5.5 collective-permute-done
  338.8 1.4 fusion.119
  345.7 2.4 conditional.25
  348.1 2.5 conditional.27
  351.0 7.5 %collective-permute-start = (bf16[2,256,128]{2,1,0:T(8,128)(2,1)S(1)}, bf16[2,256,128]{2,1,0:T(8,128)(2,1)S(1)}, u32[]{:S(2)}, u32[]{:S(2)}) collective-permute-start(bf16[2,256,128]{2,1,0:T(8,128)(2,1)S(1)} %copy.95), channel_id=1, source_target_pairs={{0,4},{4,8},{8,12},{12,16},{16,20},{20,24},{24,28},{28,0},{1,5},{5... | collective-permute-start | bytes 393224 | tf_op jit(solution)/shard_map/while/body/eval_jaxpr/ppermute | solution.py:14
  358.8 2.6 collective-permute-done
  362.0 1.4 fusion.119
  368.9 2.4 conditional.25
  371.3 2.5 conditional.27
  374.1 7.2 %collective-permute-start.1 = (f32[2,256,128]{2,1,0:T(8,128)S(1)}, f32[2,256,128]{2,1,0:T(8,128)S(1)}, u32[]{:S(2)}, u32[]{:S(2)}) collective-permute-start(f32[2,256,128]{2,1,0:T(8,128)S(1)} %pad_maximum_fusion.9), channel_id=1, source_target_pairs={{0,4},{4,8},{8,12},{12,16},{16,20},{20,24},{24,28},{28,0},{1,5},{5... | collective-permute-start | bytes 786440 | tf_op jit(solution)/shard_map/while/body/eval_jaxpr/ppermute | solution.py:14
  381.7 8.6 %collective-permute-done = bf16[2,256,128]{2,1,0:T(8,128)(2,1)S(1)} collective-permute-done((bf16[2,256,128]{2,1,0:T(8,128)(2,1)S(1)}, bf16[2,256,128]{2,1,0:T(8,128)(2,1)S(1)}, u32[]{:S(2)}, u32[]{:S(2)}) %collective-permute-start) | collective-permute-done | bytes 131104 | tf_op jit(solution)/shard_map/while/body/eval_jaxpr/ppermute | solution.py:14
  391.0 1.4 fusion.119
  398.2 8.3 %collective-permute-start.1 = (f32[2,256,128]{2,1,0:T(8,128)S(1)}, f32[2,256,128]{2,1,0:T(8,128)S(1)}, u32[]{:S(2)}, u32[]{:S(2)}) collective-permute-start(f32[2,256,128]{2,1,0:T(8,128)S(1)} %pad_maximum_fusion.9), channel_id=1, source_target_pairs={{0,4},{4,8},{8,12},{12,16},{16,20},{20,24},{24,28},{28,0},{1,5},{5... | collective-permute-start | bytes 786440 | tf_op jit(solution)/shard_map/while/body/eval_jaxpr/ppermute | solution.py:14
  407.8 7.2 %collective-permute-done = bf16[2,256,128]{2,1,0:T(8,128)(2,1)S(1)} collective-permute-done((bf16[2,256,128]{2,1,0:T(8,128)(2,1)S(1)}, bf16[2,256,128]{2,1,0:T(8,128)(2,1)S(1)}, u32[]{:S(2)}, u32[]{:S(2)}) %collective-permute-start) | collective-permute-done | bytes 131104 | tf_op jit(solution)/shard_map/while/body/eval_jaxpr/ppermute | solution.py:14
  415.7 1.4 fusion.119
  422.9 6.5 %collective-permute-start.1 = (f32[2,256,128]{2,1,0:T(8,128)S(1)}, f32[2,256,128]{2,1,0:T(8,128)S(1)}, u32[]{:S(2)}, u32[]{:S(2)}) collective-permute-start(f32[2,256,128]{2,1,0:T(8,128)S(1)} %pad_maximum_fusion.9), channel_id=1, source_target_pairs={{0,4},{4,8},{8,12},{12,16},{16,20},{20,24},{24,28},{28,0},{1,5},{5... | collective-permute-start | bytes 786440 | tf_op jit(solution)/shard_map/while/body/eval_jaxpr/ppermute | solution.py:14
  429.4 4.2 collective-permute-start
  433.9 3.2 collective-permute-done
  437.1 6.9 %convolution_bitcast_fusion.16 = f32[8192,256]{0,1:T(8,128)} fusion(bf16[1,256,8192]{2,1,0:T(8,128)(2,1)} %param.32, bf16[256,128]{1,0:T(8,128)(2,1)S(1)} %bitcast.337, bf16[256,128]{1,0:T(8,128)(2,1)S(1)} %bitcast.338), kind=kOutput, calls=%fused_computation.147 | convolution fusion | flops 1074003968 | bytes 12713984 | tf_op jit(solution)/shard_map/dot_general | solution.py:199
  445.2 178.2 %all-reduce.3.cloned.1.call-done = f32[8192,256]{0,1:T(8,128)} async-done(((f32[8192,256]{0,1:T(8,128)}), f32[8192,256]{0,1:T(8,128)}) %all-reduce.3.cloned.1.call-update) | async-done | bytes 8388624 | tf_op jit(solution)/shard_map/psum | solution.py:202
  623.3 9.0 %copy.35 = f32[8192,256]{1,0:T(8,128)} copy(f32[8192,256]{0,1:T(8,128)} %all-reduce.3.cloned.1.call-done) | data formatting | bytes 16777216
  (474 shorter events, 96.5 us)
Async XLA Ops:
  7.2 616.2 %all-reduce.3.cloned.1.call-start = ((), (), s32[]{:S(2)}) async-start(), calls=%async_computation | async-start | bytes 16777216 | tf_op jit(solution)/shard_map/psum | solution.py:202
  201.7 60.7 %collective-permute-start.1 = (f32[2,256,128]{2,1,0:T(8,128)S(1)}, f32[2,256,128]{2,1,0:T(8,128)S(1)}, u32[]{:S(2)}, u32[]{:S(2)}) collective-permute-start(f32[2,256,128]{2,1,0:T(8,128)S(1)} %pad_maximum_fusion.9), channel_id=1, source_target_pairs={{0,4},{4,8},{8,12},{12,16},{16,20},{20,24},{24,28},{28,0},{1,5},{5... | collective-permute-start | bytes 786440 | tf_op jit(solution)/shard_map/while/body/eval_jaxpr/ppermute | solution.py:14
  254.7 7.7 %collective-permute-start = (bf16[2,256,128]{2,1,0:T(8,128)(2,1)S(1)}, bf16[2,256,128]{2,1,0:T(8,128)(2,1)S(1)}, u32[]{:S(2)}, u32[]{:S(2)}) collective-permute-start(bf16[2,256,128]{2,1,0:T(8,128)(2,1)S(1)} %copy.95), channel_id=1, source_target_pairs={{0,4},{4,8},{8,12},{12,16},{16,20},{20,24},{24,28},{28,0},{1,5},{5... | collective-permute-start | bytes 393224 | tf_op jit(solution)/shard_map/while/body/eval_jaxpr/ppermute | solution.py:14
  277.4 10.5 %collective-permute-start.1 = (f32[2,256,128]{2,1,0:T(8,128)S(1)}, f32[2,256,128]{2,1,0:T(8,128)S(1)}, u32[]{:S(2)}, u32[]{:S(2)}) collective-permute-start(f32[2,256,128]{2,1,0:T(8,128)S(1)} %pad_maximum_fusion.9), channel_id=1, source_target_pairs={{0,4},{4,8},{8,12},{12,16},{16,20},{20,24},{24,28},{28,0},{1,5},{5... | collective-permute-start | bytes 786440 | tf_op jit(solution)/shard_map/while/body/eval_jaxpr/ppermute | solution.py:14
  279.9 8.0 %collective-permute-start = (bf16[2,256,128]{2,1,0:T(8,128)(2,1)S(1)}, bf16[2,256,128]{2,1,0:T(8,128)(2,1)S(1)}, u32[]{:S(2)}, u32[]{:S(2)}) collective-permute-start(bf16[2,256,128]{2,1,0:T(8,128)(2,1)S(1)} %copy.95), channel_id=1, source_target_pairs={{0,4},{4,8},{8,12},{12,16},{16,20},{20,24},{24,28},{28,0},{1,5},{5... | collective-permute-start | bytes 393224 | tf_op jit(solution)/shard_map/while/body/eval_jaxpr/ppermute | solution.py:14
  300.6 12.3 %collective-permute-start.1 = (f32[2,256,128]{2,1,0:T(8,128)S(1)}, f32[2,256,128]{2,1,0:T(8,128)S(1)}, u32[]{:S(2)}, u32[]{:S(2)}) collective-permute-start(f32[2,256,128]{2,1,0:T(8,128)S(1)} %pad_maximum_fusion.9), channel_id=1, source_target_pairs={{0,4},{4,8},{8,12},{12,16},{16,20},{20,24},{24,28},{28,0},{1,5},{5... | collective-permute-start | bytes 786440 | tf_op jit(solution)/shard_map/while/body/eval_jaxpr/ppermute | solution.py:14
  305.2 7.7 %collective-permute-start = (bf16[2,256,128]{2,1,0:T(8,128)(2,1)S(1)}, bf16[2,256,128]{2,1,0:T(8,128)(2,1)S(1)}, u32[]{:S(2)}, u32[]{:S(2)}) collective-permute-start(bf16[2,256,128]{2,1,0:T(8,128)(2,1)S(1)} %copy.95), channel_id=1, source_target_pairs={{0,4},{4,8},{8,12},{12,16},{16,20},{20,24},{24,28},{28,0},{1,5},{5... | collective-permute-start | bytes 393224 | tf_op jit(solution)/shard_map/while/body/eval_jaxpr/ppermute | solution.py:14
  323.2 15.0 %collective-permute-start.1 = (f32[2,256,128]{2,1,0:T(8,128)S(1)}, f32[2,256,128]{2,1,0:T(8,128)S(1)}, u32[]{:S(2)}, u32[]{:S(2)}) collective-permute-start(f32[2,256,128]{2,1,0:T(8,128)S(1)} %pad_maximum_fusion.9), channel_id=1, source_target_pairs={{0,4},{4,8},{8,12},{12,16},{16,20},{20,24},{24,28},{28,0},{1,5},{5... | collective-permute-start | bytes 786440 | tf_op jit(solution)/shard_map/while/body/eval_jaxpr/ppermute | solution.py:14
  330.5 7.7 %collective-permute-start = (bf16[2,256,128]{2,1,0:T(8,128)(2,1)S(1)}, bf16[2,256,128]{2,1,0:T(8,128)(2,1)S(1)}, u32[]{:S(2)}, u32[]{:S(2)}) collective-permute-start(bf16[2,256,128]{2,1,0:T(8,128)(2,1)S(1)} %copy.95), channel_id=1, source_target_pairs={{0,4},{4,8},{8,12},{12,16},{16,20},{20,24},{24,28},{28,0},{1,5},{5... | collective-permute-start | bytes 393224 | tf_op jit(solution)/shard_map/while/body/eval_jaxpr/ppermute | solution.py:14
  350.8 10.5 %collective-permute-start.1 = (f32[2,256,128]{2,1,0:T(8,128)S(1)}, f32[2,256,128]{2,1,0:T(8,128)S(1)}, u32[]{:S(2)}, u32[]{:S(2)}) collective-permute-start(f32[2,256,128]{2,1,0:T(8,128)S(1)} %pad_maximum_fusion.9), channel_id=1, source_target_pairs={{0,4},{4,8},{8,12},{12,16},{16,20},{20,24},{24,28},{28,0},{1,5},{5... | collective-permute-start | bytes 786440 | tf_op jit(solution)/shard_map/while/body/eval_jaxpr/ppermute | solution.py:14
  351.0 10.4 %collective-permute-start = (bf16[2,256,128]{2,1,0:T(8,128)(2,1)S(1)}, bf16[2,256,128]{2,1,0:T(8,128)(2,1)S(1)}, u32[]{:S(2)}, u32[]{:S(2)}) collective-permute-start(bf16[2,256,128]{2,1,0:T(8,128)(2,1)S(1)} %copy.95), channel_id=1, source_target_pairs={{0,4},{4,8},{8,12},{12,16},{16,20},{20,24},{24,28},{28,0},{1,5},{5... | collective-permute-start | bytes 393224 | tf_op jit(solution)/shard_map/while/body/eval_jaxpr/ppermute | solution.py:14
  374.1 16.2 %collective-permute-start.1 = (f32[2,256,128]{2,1,0:T(8,128)S(1)}, f32[2,256,128]{2,1,0:T(8,128)S(1)}, u32[]{:S(2)}, u32[]{:S(2)}) collective-permute-start(f32[2,256,128]{2,1,0:T(8,128)S(1)} %pad_maximum_fusion.9), channel_id=1, source_target_pairs={{0,4},{4,8},{8,12},{12,16},{16,20},{20,24},{24,28},{28,0},{1,5},{5... | collective-permute-start | bytes 786440 | tf_op jit(solution)/shard_map/while/body/eval_jaxpr/ppermute | solution.py:14
  381.3 9.0 %collective-permute-start = (bf16[2,256,128]{2,1,0:T(8,128)(2,1)S(1)}, bf16[2,256,128]{2,1,0:T(8,128)(2,1)S(1)}, u32[]{:S(2)}, u32[]{:S(2)}) collective-permute-start(bf16[2,256,128]{2,1,0:T(8,128)(2,1)S(1)} %copy.95), channel_id=1, source_target_pairs={{0,4},{4,8},{8,12},{12,16},{16,20},{20,24},{24,28},{28,0},{1,5},{5... | collective-permute-start | bytes 393224 | tf_op jit(solution)/shard_map/while/body/eval_jaxpr/ppermute | solution.py:14
  398.2 16.8 %collective-permute-start.1 = (f32[2,256,128]{2,1,0:T(8,128)S(1)}, f32[2,256,128]{2,1,0:T(8,128)S(1)}, u32[]{:S(2)}, u32[]{:S(2)}) collective-permute-start(f32[2,256,128]{2,1,0:T(8,128)S(1)} %pad_maximum_fusion.9), channel_id=1, source_target_pairs={{0,4},{4,8},{8,12},{12,16},{16,20},{20,24},{24,28},{28,0},{1,5},{5... | collective-permute-start | bytes 786440 | tf_op jit(solution)/shard_map/while/body/eval_jaxpr/ppermute | solution.py:14
  406.5 8.5 %collective-permute-start = (bf16[2,256,128]{2,1,0:T(8,128)(2,1)S(1)}, bf16[2,256,128]{2,1,0:T(8,128)(2,1)S(1)}, u32[]{:S(2)}, u32[]{:S(2)}) collective-permute-start(bf16[2,256,128]{2,1,0:T(8,128)(2,1)S(1)} %copy.95), channel_id=1, source_target_pairs={{0,4},{4,8},{8,12},{12,16},{16,20},{20,24},{24,28},{28,0},{1,5},{5... | collective-permute-start | bytes 393224 | tf_op jit(solution)/shard_map/while/body/eval_jaxpr/ppermute | solution.py:14
  422.9 14.2 %collective-permute-start.1 = (f32[2,256,128]{2,1,0:T(8,128)S(1)}, f32[2,256,128]{2,1,0:T(8,128)S(1)}, u32[]{:S(2)}, u32[]{:S(2)}) collective-permute-start(f32[2,256,128]{2,1,0:T(8,128)S(1)} %pad_maximum_fusion.9), channel_id=1, source_target_pairs={{0,4},{4,8},{8,12},{12,16},{16,20},{20,24},{24,28},{28,0},{1,5},{5... | collective-permute-start | bytes 786440 | tf_op jit(solution)/shard_map/while/body/eval_jaxpr/ppermute | solution.py:14
  429.4 7.7 %collective-permute-start = (bf16[2,256,128]{2,1,0:T(8,128)(2,1)S(1)}, bf16[2,256,128]{2,1,0:T(8,128)(2,1)S(1)}, u32[]{:S(2)}, u32[]{:S(2)}) collective-permute-start(bf16[2,256,128]{2,1,0:T(8,128)(2,1)S(1)} %copy.95), channel_id=1, source_target_pairs={{0,4},{4,8},{8,12},{12,16},{16,20},{20,24},{24,28},{28,0},{1,5},{5... | collective-permute-start | bytes 393224 | tf_op jit(solution)/shard_map/while/body/eval_jaxpr/ppermute | solution.py:14
  437.1 7.0 %copy-start = (bf16[1,256,128]{2,1,0:T(8,128)(2,1)}, bf16[1,256,128]{2,1,0:T(8,128)(2,1)S(1)}, u32[]{:S(2)}) copy-start(bf16[1,256,128]{2,1,0:T(8,128)(2,1)S(1)} %get-tuple-element.902) | copy-start | bytes 196612
  437.1 7.0 %copy-start.1 = (bf16[1,256,128]{2,1,0:T(8,128)(2,1)}, bf16[1,256,128]{2,1,0:T(8,128)(2,1)S(1)}, u32[]{:S(2)}) copy-start(bf16[1,256,128]{2,1,0:T(8,128)(2,1)S(1)} %get-tuple-element.903) | copy-start | bytes 196612
Sparse Core Ops, SparseCore 0:
  444.2 179.0 all-reduce.2
where the time goes:
time: 643 us; the launch traced here: 639 us
  waiting for transfers between devices  227 us (35%)
  loops' own time  121 us (19%)
  starting transfers between devices  105 us (16%)
  local copies, waits for them, and re-layouts  69.8 us (11%)
  blocking collectives  44.8 us (7%)
  other arithmetic  34.9 us (5%)
  matrix products  22 us (3%)
  between operations  14.8 us (2%)
    psum x1, waiting for transfers between devices, local(): grad_weights = lax.psum(partial_weights, ('ctx', 'dp'))  178 us
    ppermute x16, starting transfers between devices, from_behind(): return lax.ppermute(value, axis, pairs)  105 us
    ppermute x16, waiting for transfers between devices, from_behind(): return lax.ppermute(value, axis, pairs)  48.4 us
    another operation x1, loops' own time, local(): lax.fori_loop(0, cycle_size, cycle_step, (key_value, grad_start, query_st...  43.6 us
    another operation x1, loops' own time, local(): lax.fori_loop(0, shard_rows.shape[1] // tokens_dev, one_shard, start_stats)  41.2 us
    all_gather x1, blocking collectives, local(): shard_rows = lax.all_gather(key, 'ctx', axis=1, tiled=True)  31.7 us
    another operation x32, loops' own time, visit(): lax.cond(key_block <= query_blocks[slot_q], partial(tile_terms, queries[s...  18.9 us
    another operation x32, loops' own time, stats_update(): lax.cond(key_block <= query_blocks[slot_q], partial(stats_tile, queries[s...  17.3 us
  transfers between devices with their start and end apart: 17, of which 9 were waited for; matrix products, arithmetic and copies ran while one was open for 1% of the time, Pallas kernels for 0%

commit v1 on v0

v1 whole, which is shorter than its diff:
```python
import functools

import jax
import jax.numpy as jnp
from jax import lax
from jax.experimental import pallas as pl
from jax.experimental.pallas import tpu as pltpu
from jax.sharding import PartitionSpec as P

NEG_FILL = -1e30
LOG2_E = 1.4426950408889634


def dot_nt(left, right):
    return lax.dot_general(left, right, (((1,), (1,)), ((), ())), preferred_element_type=jnp.float32)


def dot_nn(left, right):
    return lax.dot_general(left, right, (((1,), (0,)), ((), ())), preferred_element_type=jnp.float32)


def dot_tn(left, right):
    return lax.dot_general(left, right, (((0,), (0,)), ((), ())), preferred_element_type=jnp.float32)


def attention_kernel(
    chunks, heads, width, block,
    table_ref, own_ref, q_ref, g_ref, o_ref, kv_ref,
    dq_ref, dkv_ref, s_ref, acc_ref,
):
    rows = heads * block
    tokens = 2 * block
    scale = width ** -0.5
    key_row = lax.broadcasted_iota(jnp.int32, (block, rows), 0)
    query_col = lax.rem(lax.broadcasted_iota(jnp.int32, (block, rows), 1), block)
    gap = key_row - query_col
    for slot in range(2):

        def stacked(ref):
            part = ref[slot * block:(slot + 1) * block, :]
            return jnp.concatenate([part[:, h * width:(h + 1) * width] for h in range(heads)], axis=0)

        queries, grads = stacked(q_ref), stacked(g_ref)
        product = grads.astype(jnp.float32) * stacked(o_ref).astype(jnp.float32)
        delta = jnp.sum(jnp.transpose(product), axis=0, keepdims=True) * scale
        own = own_ref[slot]

        def score_step(chunk, high):
            base = pl.multiple_of(chunk * tokens, tokens)
            scores = dot_nt(kv_ref[pl.ds(base, tokens), :width], queries) * (scale * LOG2_E)
            for half in range(2):
                ahead = (own - table_ref[2 * chunk + half]) * block
                piece = jnp.where(gap <= ahead, scores[half * block:(half + 1) * block, :], NEG_FILL)
                s_ref[pl.ds(pl.multiple_of(base + half * block, block), block), :] = piece
                high = jnp.maximum(high, jnp.max(piece.reshape(block // 8, 8, rows), axis=0))
            return high

        high = lax.fori_loop(0, chunks, score_step, jnp.full((8, rows), NEG_FILL, jnp.float32))
        top = jnp.max(high, axis=0, keepdims=True)

        def exp_step(chunk, total):
            at = pl.ds(pl.multiple_of(chunk * tokens, tokens), tokens)
            weights = jnp.exp2(s_ref[at, :] - top)
            s_ref[at, :] = weights
            return total + jnp.sum(weights.reshape(tokens // 8, 8, rows), axis=0)

        total = lax.fori_loop(0, chunks, exp_step, jnp.zeros((8, rows), jnp.float32))
        inverse = 1.0 / jnp.sum(total, axis=0, keepdims=True)

        def grad_step(chunk, query_sum):
            at = pl.ds(pl.multiple_of(chunk * tokens, tokens), tokens)
            keys, values = kv_ref[at, :width], kv_ref[at, width:]
            probs = s_ref[at, :] * inverse
            prob_grads = dot_nt(values, grads)
            score_grads = (probs * (prob_grads * scale - delta)).astype(jnp.bfloat16)
            value_add = dot_nn(probs.astype(jnp.bfloat16), grads)
            key_add = dot_nn(score_grads, queries)
            if slot == 0:
                acc_ref[at, :width] = key_add
                acc_ref[at, width:] = value_add
            else:
                dkv_ref[at, :width] = (acc_ref[at, :width] + key_add).astype(jnp.bfloat16)
                dkv_ref[at, width:] = (acc_ref[at, width:] + value_add).astype(jnp.bfloat16)
            return query_sum + dot_tn(keys, score_grads)

        query_sum = lax.fori_loop(0, chunks, grad_step, jnp.zeros((width, rows), jnp.float32))
        for h in range(heads):
            dq_ref[slot * block:(slot + 1) * block, h * width:(h + 1) * width] = jnp.transpose(
                query_sum[:, h * block:(h + 1) * block]
            ).astype(jnp.bfloat16)


def attention(table, own, query, out_grad, output, key_value, width):
    tokens_dev, wide = query.shape
    length = key_value.shape[0]
    block = tokens_dev // 2
    heads = wide // width
    smem = pl.BlockSpec(memory_space=pltpu.SMEM)
    vmem = pl.BlockSpec(memory_space=pltpu.VMEM)
    return pl.pallas_call(
        functools.partial(attention_kernel, length // tokens_dev, heads, width, block),
        out_shape=(
            jax.ShapeDtypeStruct((tokens_dev, wide), jnp.bfloat16),
            jax.ShapeDtypeStruct((length, 2 * width), jnp.bfloat16),
        ),
        in_specs=[smem, smem, vmem, vmem, vmem, vmem],
        out_specs=(vmem, vmem),
        scratch_shapes=[
            pltpu.VMEM((length, heads * block), jnp.float32),
            pltpu.VMEM((length, 2 * width), jnp.float32),
        ],
        compiler_params=pltpu.CompilerParams(vmem_limit_bytes=48 * 1024 * 1024),
        cost_estimate=pl.CostEstimate(
            flops=10 * tokens_dev * wide * length, bytes_accessed=4 * length * wide, transcendentals=0
        ),
    )(table, own, query, out_grad, output, key_value)


def local(query, key, value, out_grad, output, inputs, span_ids):
    tokens_dev, width = key.shape[1], key.shape[2]
    count = lax.axis_size("ctx")
    table = lax.all_gather(span_ids, "ctx", axis=0, tiled=True)
    own_pair = jnp.concatenate([key[0], value[0]], axis=1)
    key_value = lax.all_gather(own_pair, "ctx", axis=0, tiled=True)
    query_low, grads = attention(table, span_ids, query[0], out_grad[0], output[0], key_value, width)
    terms = lax.all_to_all(grads.reshape(count, tokens_dev, 2 * width), "ctx", 0, 0)
    pair = jnp.sum(terms.astype(jnp.float32), axis=0).astype(jnp.bfloat16)
    partial_weights = lax.dot_general(
        inputs[0], pair, (((0,), (0,)), ((), ())), preferred_element_type=jnp.float32
    )
    part = lax.psum_scatter(partial_weights, ("ctx", "dp"), scatter_dimension=0, tiled=True)
    weights = lax.all_gather(part.astype(jnp.bfloat16), ("ctx", "dp"), axis=0, tiled=True)
    weights = weights.astype(jnp.float32)
    return (query_low[None], pair[None, :, :width], pair[None, :, width:], weights)


def solution(mesh):
    row = P("dp", "ctx", None)
    return jax.shard_map(
        local,
        mesh=mesh,
        in_specs=(row, row, row, row, row, row, P("ctx")),
        out_specs=(row, row, row, P()),
        check_vma=False,
    )
```

time: 643 us -> 335 us (0.52)
  loops' own time: 121 us -> 0 us
  starting transfers between devices: 105 us -> 0.12 us
  local copies, waits for them, and re-layouts: 69.8 us -> 14.5 us
  other arithmetic: 34.9 us -> 3.31 us
  matrix products: 22 us -> 6.87 us
  Pallas kernels: 0 us -> 13.5 us
  waiting for transfers between devices: 227 us -> 240 us
    psum x1 -> x0, waiting for transfers between devices: 178 us -> none  [local(): grad_weights = lax.psum(partial_weights, ('ctx', 'dp'))]
    reduce_scatter x0 -> x1, waiting for transfers between devices: none -> 148 us  [local(): lax.psum_scatter(partial_weights, ('ctx', 'dp'), scatter_dimension=0, til...]
    another operation x66 -> x0, loops' own time: 121 us -> none  [the longest x1 43.6 us: local(): lax.fori_loop(0, cycle_size, cycle_step, (key_value, grad_start, query_st...]
    ppermute x16 -> x0, starting transfers between devices: 105 us -> none  [from_behind(): return lax.ppermute(value, axis, pairs)]
    all_gather x0 -> x2, waiting for transfers between devices: none -> 92.4 us  [the longest x1 63.6 us: local(): lax.all_gather(part.astype(jnp.bfloat16), ('ctx', 'dp'), axis=0, tiled=True)]
    ppermute x16 -> x0, waiting for transfers between devices: 48.4 us -> none  [from_behind(): return lax.ppermute(value, axis, pairs)]
    slice x41 -> x0, local copies, waits for them, and re-layouts: 32.3 us -> none  [the longest x8 11.1 us: visit(): query_blocks[slot_q]]
    all_gather x1 -> x0, blocking collectives: 31.7 us -> none  [local(): shard_rows = lax.all_gather(key, 'ctx', axis=1, tiled=True)]
  transfers between devices with their start and end apart: 17 -> 3, of which waited for: 9 -> 3; matrix products, arithmetic and copies ran while one was open for 1% -> 1% of each run, Pallas kernels for 0% -> 0%
where the time goes in v1:
time: 335 us; the launch traced here: 334 us
  waiting for transfers between devices  240 us (72%)
  blocking collectives  40.6 us (12%)
  local copies, waits for them, and re-layouts  14.5 us (4%)
  between operations  14.4 us (4%)
  Pallas kernels  13.5 us (4%)
  matrix products  6.87 us (2%)
    reduce_scatter x1, waiting for transfers between devices, local(): lax.psum_scatter(partial_weights, ('ctx', 'dp'), scatter_dimension=0, til...  148 us
    all_gather x1, waiting for transfers between devices, local(): lax.all_gather(part.astype(jnp.bfloat16), ('ctx', 'dp'), axis=0, tiled=True)  63.6 us
    all_gather x1, waiting for transfers between devices, local(): key_value = lax.all_gather(own_pair, 'ctx', axis=0, tiled=True)  28.8 us
    all_to_all x1, blocking collectives, local(): lax.all_to_all(grads.reshape(count, tokens_dev, 2 * width), 'ctx', 0, 0)  27.5 us
    unnamed x14, local copies, waits for them, and re-layouts  13.8 us
    pallas_call x1, Pallas kernels, attention(): pl.pallas_call(functools.partial(attention_kernel, length // tokens_dev,...  13.5 us
    unnamed x1, blocking collectives  13.2 us
    dot_general x1, matrix products, local(): lax.dot_general(inputs[0], pair, (((0,), (0,)), ((), ())), preferred_elem...  6.87 us
  transfers between devices with their start and end apart: 3, of which 3 were waited for; matrix products, arithmetic and copies ran while one was open for 1% of the time, Pallas kernels for 0%

profile of v1, /device:TPU:0, one launch (start us, length us, event | category | flops | bytes accessed | tf_op | source)
XLA Modules:
  0.0 333.8 jit_solution(12941880704270602998)
XLA Ops:
  7.2 0.0 all-gather.3.cloned.1.call-start
  7.2 1.5 pad_maximum_fusion
  8.8 0.0 all-gather.3.cloned.1.call-update
  8.8 0.0 reduce-scatter.2.cloned.1.call-start
  8.8 1.2 dynamic-slice
  10.7 0.9 dynamic-update-slice
  11.6 13.2 %all-reduce.table_ref = s32[16]{0:T(128)S(1)} all-reduce(s32[16]{0:T(128)S(1)} %dynamic-update-slice), channel_id=1, replica_groups=mesh['ctx'=8,'dp'=4] {'ctx'}, use_global_device_ids=true, to_apply=%add | all-reduce | flops 16 | bytes 128
  24.8 28.8 %all-gather.3.cloned.1.call-done.kv_ref = bf16[2048,256]{1,0:T(8,128)(2,1)} async-done(((bf16[256,256]{1,0:T(8,128)(2,1)}), bf16[2048,256]{1,0:T(8,128)(2,1)}) %all-gather.3.cloned.1.call-update) | async-done | bytes 1048592 | tf_op jit(solution)/shard_map/all_gather | solution.py:124
  53.6 0.0 copy-start
  53.6 1.2 copy-done
  54.8 0.0 copy-start.1
  54.8 0.9 copy-done.1
  55.8 0.0 copy-start.2
  55.8 0.9 copy-done.2
  56.7 0.0 copy-start.3
  56.7 0.9 copy-done.3
  57.7 0.0 copy-start.4
  57.7 0.7 copy-done.4
  58.3 13.5 %shard_map.102 = (bf16[256,512]{1,0:T(8,128)(2,1)}, bf16[2048,256]{1,0:T(8,128)(2,1)S(1)}) custom-call(s32[16]{0:T(128)S(1)} %all-reduce.table_ref, s32[2]{0:T(128)S(1)} %copy-done.4, bf16[256,512]{1,0:T(8,128)(2,1)S(1)} %bitcast.19, bf16[256,512]{1,0:T(8,128)(2,1)S(1)} %bitcast.20, bf16[256,512]{1,0:T(8,128)(2,1)S(1)} %bitcast.21, bf16[2048,256]{1,0:T(8,128)(2,1)S(1)} %copy-done), custom_call_target="tpu_custom_call" | custom-call | flops 2684354560 | bytes 4194304 | tf_op jit(solution)/shard_map/pallas_call | solution.py:100
  71.8 27.5 %all_to_all.5 = bf16[8,256,256]{2,1,0:T(8,128)(2,1)S(1)} all-to-all(bf16[8,256,256]{2,1,0:T(8,128)(2,1)S(1)} %bitcast.18), channel_id=1, replica_groups=mesh['ctx'=8,'dp'=4] {'ctx'}, dimensions={0} | all-to-all | bytes 2097152 | tf_op jit(solution)/shard_map/all_to_all | solution.py:126
  99.3 0.1 reduce_sum.12
  99.4 6.9 %convolution_bitcast_fusion = f32[8192,256]{0,1:T(8,128)} fusion(bf16[256,256]{1,0:T(8,128)(2,1)S(1)} %reduce_sum.12, bf16[1,256,8192]{2,1,0:T(8,128)(2,1)} %param.12), kind=kOutput, calls=%fused_computation | convolution fusion | flops 1073741824 | bytes 12713984 | tf_op jit(solution)/shard_map/dot_general | solution.py:128
  106.3 0.0 reduce-scatter.2.cloned.1.call-update
  106.3 0.0 all-gather.5.cloned.1.call-start
  106.4 148.0 %reduce-scatter.2.cloned.1.call-done = f32[256,256]{0,1:T(8,128)} async-done(((f32[8192,256]{0,1:T(8,128)}), f32[256,256]{0,1:T(8,128)}) %reduce-scatter.2.cloned.1.call-update) | async-done | bytes 262160 | tf_op jit(solution)/shard_map/reduce_scatter | solution.py:131
  254.4 1.6 convert_element_type.8
  256.0 0.0 all-gather.5.cloned.1.call-update
  256.0 0.7 slice_bitcast_fusion
  256.7 63.6 %all-gather.5.cloned.1.call-done = bf16[8192,256]{0,1:T(8,128)(2,1)} async-done(((bf16[256,256]{0,1:T(8,128)(2,1)}), bf16[8192,256]{0,1:T(8,128)(2,1)}) %all-gather.5.cloned.1.call-update) | async-done | bytes 4194320 | tf_op jit(solution)/shard_map/all_gather | solution.py:132
  320.3 7.0 %copy.11 = f32[8192,256]{1,0:T(8,128)} copy(bf16[8192,256]{0,1:T(8,128)(2,1)} %all-gather.5.cloned.1.call-done) | data formatting | bytes 12582912
  (1 shorter events, 0.0 us)
Async XLA Ops:
  7.2 46.4 %all-gather.3.cloned.1.call-start = ((), (), s32[]{:S(2)}) async-start(), calls=%async_computation.2 | async-start | bytes 1179648 | tf_op jit(solution)/shard_map/all_gather | solution.py:124
  8.8 245.6 %reduce-scatter.2.cloned.1.call-start = ((), (), s32[]{:S(2)}) async-start(), calls=%async_computation.3 | async-start | bytes 8650752 | tf_op jit(solution)/shard_map/reduce_scatter | solution.py:131
  53.6 1.2 copy-start
  54.8 0.9 copy-start.1
  55.8 0.9 copy-start.2
  56.7 0.9 copy-start.3
  57.7 0.7 copy-start.4
  106.3 214.0 %all-gather.5.cloned.1.call-start = ((), (), s32[]{:S(2)}) async-start(), calls=%async_computation.4 | async-start | bytes 4325376 | tf_op jit(solution)/shard_map/all_gather | solution.py:132
Sparse Core Ops, SparseCore 0:
  10.7 42.8 all-gather.2
  106.5 147.8 reduce-scatter.1
  257.8 62.4 all-gather.4

commit v2 on v1

--- a/solution.py
+++ b/solution.py
@@ -24,7 +24,7 @@
 
 
 def attention_kernel(
-    chunks, heads, width, block,
+    chunks, heads, width, block, stride,
     table_ref, own_ref, q_ref, g_ref, o_ref, kv_ref,
     dq_ref, dkv_ref, s_ref, acc_ref,
 ):
@@ -47,7 +47,7 @@
 
         def score_step(chunk, high):
             base = pl.multiple_of(chunk * tokens, tokens)
-            scores = dot_nt(kv_ref[pl.ds(base, tokens), :width], queries) * (scale * LOG2_E)
+            scores = dot_nt(kv_ref[pl.ds(pl.multiple_of(chunk * stride, 16), tokens), :width], queries) * (scale * LOG2_E)
             for half in range(2):
                 ahead = (own - table_ref[2 * chunk + half]) * block
                 piece = jnp.where(gap <= ahead, scores[half * block:(half + 1) * block, :], NEG_FILL)
@@ -69,7 +69,8 @@
 
         def grad_step(chunk, query_sum):
             at = pl.ds(pl.multiple_of(chunk * tokens, tokens), tokens)
-            keys, values = kv_ref[at, :width], kv_ref[at, width:]
+            held = pl.ds(pl.multiple_of(chunk * stride, 16), tokens)
+            keys, values = kv_ref[held, :width], kv_ref[held, width:]
             probs = s_ref[at, :] * inverse
             prob_grads = dot_nt(values, grads)
             score_grads = (probs * (prob_grads * scale - delta)).astype(jnp.bfloat16)
@@ -90,15 +91,16 @@
             ).astype(jnp.bfloat16)
 
 
-def attention(table, own, query, out_grad, output, key_value, width):
+def attention(table, own, query, out_grad, output, key_value, width, stride):
     tokens_dev, wide = query.shape
-    length = key_value.shape[0]
+    chunks = key_value.shape[0] // stride
+    length = chunks * tokens_dev
     block = tokens_dev // 2
     heads = wide // width
     smem = pl.BlockSpec(memory_space=pltpu.SMEM)
     vmem = pl.BlockSpec(memory_space=pltpu.VMEM)
     return pl.pallas_call(
-        functools.partial(attention_kernel, length // tokens_dev, heads, width, block),
+        functools.partial(attention_kernel, chunks, heads, width, block, stride),
         out_shape=(
             jax.ShapeDtypeStruct((tokens_dev, wide), jnp.bfloat16),
             jax.ShapeDtypeStruct((length, 2 * width), jnp.bfloat16),
@@ -119,18 +121,20 @@
 def local(query, key, value, out_grad, output, inputs, span_ids):
     tokens_dev, width = key.shape[1], key.shape[2]
     count = lax.axis_size("ctx")
-    table = lax.all_gather(span_ids, "ctx", axis=0, tiled=True)
-    own_pair = jnp.concatenate([key[0], value[0]], axis=1)
+    stride = tokens_dev + 16
+    numbers = jnp.pad(span_ids.astype(jnp.bfloat16)[None, :], ((0, 15), (0, 2 * width - 2)))
+    own_pair = jnp.concatenate([jnp.concatenate([key[0], value[0]], axis=1), numbers], axis=0)
     key_value = lax.all_gather(own_pair, "ctx", axis=0, tiled=True)
-    query_low, grads = attention(table, span_ids, query[0], out_grad[0], output[0], key_value, width)
+    table = key_value.reshape(count, stride, 2 * width)[:, tokens_dev, :2].astype(jnp.int32).reshape(-1)
+    query_low, grads = attention(
+        table, span_ids, query[0], out_grad[0], output[0], key_value, width, stride
+    )
     terms = lax.all_to_all(grads.reshape(count, tokens_dev, 2 * width), "ctx", 0, 0)
     pair = jnp.sum(terms.astype(jnp.float32), axis=0).astype(jnp.bfloat16)
     partial_weights = lax.dot_general(
         inputs[0], pair, (((0,), (0,)), ((), ())), preferred_element_type=jnp.float32
     )
-    part = lax.psum_scatter(partial_weights, ("ctx", "dp"), scatter_dimension=0, tiled=True)
-    weights = lax.all_gather(part.astype(jnp.bfloat16), ("ctx", "dp"), axis=0, tiled=True)
-    weights = weights.astype(jnp.float32)
+    weights = lax.psum(partial_weights, ("ctx", "dp"))
     return (query_low[None], pair[None, :, :width], pair[None, :, width:], weights)
 
 

time: 335 us -> 302 us (0.901)
  waiting for transfers between devices: 240 us -> 222 us
  blocking collectives: 40.6 us -> 27.5 us
    psum x0 -> x1, waiting for transfers between devices: none -> 177 us  [local(): weights = lax.psum(partial_weights, ('ctx', 'dp'))]
    reduce_scatter x1 -> x0, waiting for transfers between devices: 148 us -> none  [local(): lax.psum_scatter(partial_weights, ('ctx', 'dp'), scatter_dimension=0, til...]
    all_gather x1 -> x0, waiting for transfers between devices: 63.6 us -> none  [local(): lax.all_gather(part.astype(jnp.bfloat16), ('ctx', 'dp'), axis=0, tiled=True)]
    all_gather x1, waiting for transfers between devices: 28.8 us -> 44.6 us  [local(): key_value = lax.all_gather(own_pair, 'ctx', axis=0, tiled=True)]
    unnamed x1 -> x0, blocking collectives: 13.2 us -> none
    unnamed x14 -> x11, local copies, waits for them, and re-layouts: 13.8 us -> 13.7 us
  transfers between devices with their start and end apart: 3 -> 2, of which waited for: 3 -> 2; matrix products, arithmetic and copies ran while one was open for 1% -> 0% of each run, Pallas kernels for 0% -> 0%
where the time goes in v2:
time: 302 us; the launch traced here: 301 us
  waiting for transfers between devices  222 us (74%)
  blocking collectives  27.5 us (9%)
  local copies, waits for them, and re-layouts  15.2 us (5%)
  between operations  14 us (5%)
  Pallas kernels  13.5 us (4%)
  matrix products  6.86 us (2%)
    psum x1, waiting for transfers between devices, local(): weights = lax.psum(partial_weights, ('ctx', 'dp'))  177 us
    all_gather x1, waiting for transfers between devices, local(): key_value = lax.all_gather(own_pair, 'ctx', axis=0, tiled=True)  44.6 us
    all_to_all x1, blocking collectives, local(): lax.all_to_all(grads.reshape(count, tokens_dev, 2 * width), 'ctx', 0, 0)  27.5 us
    unnamed x11, local copies, waits for them, and re-layouts  13.7 us
    pallas_call x1, Pallas kernels, attention(): pl.pallas_call(functools.partial(attention_kernel, chunks, heads, width,...  13.5 us
    dot_general x1, matrix products, local(): lax.dot_general(inputs[0], pair, (((0,), (0,)), ((), ())), preferred_elem...  6.86 us
  transfers between devices with their start and end apart: 2, of which 2 were waited for; matrix products, arithmetic and copies ran while one was open for 0% of the time, Pallas kernels for 0%

profile of v2, /device:TPU:0, one launch (start us, length us, event | category | flops | bytes accessed | tf_op | source)
XLA Modules:
  0.0 301.3 jit_solution(16899769541492406334)
XLA Ops:
  7.2 0.0 all-gather.2.cloned.1.call-start
  7.2 0.7 convert_bitcast_fusion
  7.9 1.5 fusion.2
  9.4 0.0 all-gather.2.cloned.1.call-update
  9.4 0.0 all-reduce.3.cloned.1.call-start
  9.5 44.6 %all-gather.2.cloned.1.call-done.kv_ref = bf16[2176,256]{1,0:T(8,128)(2,1)} async-done(((bf16[272,256]{1,0:T(8,128)(2,1)}), bf16[2176,256]{1,0:T(8,128)(2,1)}) %all-gather.2.cloned.1.call-update) | async-done | bytes 1114128 | tf_op jit(solution)/shard_map/all_gather | solution.py:127
  54.1 0.7 slice.12
  54.8 0.1 reshape.20.table_ref
  54.9 0.0 copy-start
  54.9 1.2 copy-done
  56.2 0.0 copy-start.1
  56.2 0.9 copy-done.1
  57.1 0.0 copy-start.2
  57.1 0.9 copy-done.2
  58.1 0.0 copy-start.3
  58.1 0.9 copy-done.3
  59.0 0.0 copy-start.4
  59.0 0.7 copy-done.4
  59.7 13.5 %shard_map.102 = (bf16[256,512]{1,0:T(8,128)(2,1)}, bf16[2048,256]{1,0:T(8,128)(2,1)S(1)}) custom-call(s32[16]{0:T(128)S(1)} %reshape.20.table_ref, s32[2]{0:T(128)S(1)} %copy-done.4, bf16[256,512]{1,0:T(8,128)(2,1)S(1)} %bitcast.24, bf16[256,512]{1,0:T(8,128)(2,1)S(1)} %bitcast.25, bf16[256,512]{1,0:T(8,128)(2,1)S(1)} %bitcast.26, bf16[2176,256]{1,0:T(8,128)(2,1)S(1)} %copy-done), custom_call_target="tpu_custom_call" | custom-call | flops 2684354560 | bytes 4194304 | tf_op jit(solution)/shard_map/pallas_call | solution.py:102
  73.2 27.5 %all_to_all.5 = bf16[8,256,256]{2,1,0:T(8,128)(2,1)S(1)} all-to-all(bf16[8,256,256]{2,1,0:T(8,128)(2,1)S(1)} %bitcast.22), channel_id=1, replica_groups=mesh['ctx'=8,'dp'=4] {'ctx'}, dimensions={0} | all-to-all | bytes 2097152 | tf_op jit(solution)/shard_map/all_to_all | solution.py:132
  100.7 0.1 reduce_sum.12
  100.8 6.9 %convolution_bitcast_fusion = f32[8192,256]{0,1:T(8,128)} fusion(bf16[256,256]{1,0:T(8,128)(2,1)S(1)} %reduce_sum.12, bf16[1,256,8192]{2,1,0:T(8,128)(2,1)} %param.12), kind=kOutput, calls=%fused_computation | convolution fusion | flops 1073741824 | bytes 12713984 | tf_op jit(solution)/shard_map/dot_general | solution.py:134
  107.7 0.0 all-reduce.3.cloned.1.call-update
  107.7 0.7 slice_bitcast_fusion
  108.4 177.1 %all-reduce.3.cloned.1.call-done = f32[8192,256]{0,1:T(8,128)} async-done(((f32[8192,256]{0,1:T(8,128)}), f32[8192,256]{0,1:T(8,128)}) %all-reduce.3.cloned.1.call-update) | async-done | bytes 8388624 | tf_op jit(solution)/shard_map/psum | solution.py:137
  285.5 9.0 %copy.14 = f32[8192,256]{1,0:T(8,128)} copy(f32[8192,256]{0,1:T(8,128)} %all-reduce.3.cloned.1.call-done) | data formatting | bytes 16777216
  (1 shorter events, 0.0 us)
Async XLA Ops:
  7.2 46.9 %all-gather.2.cloned.1.call-start = ((), (), s32[]{:S(2)}) async-start(), calls=%async_computation.1 | async-start | bytes 1253376 | tf_op jit(solution)/shard_map/all_gather | solution.py:127
  9.4 276.1 %all-reduce.3.cloned.1.call-start = ((), (), s32[]{:S(2)}) async-start(), calls=%async_computation.2 | async-start | bytes 16777216 | tf_op jit(solution)/shard_map/psum | solution.py:137
  54.9 1.3 copy-start
  56.2 0.9 copy-start.1
  57.1 0.9 copy-start.2
  58.1 0.9 copy-start.3
  59.0 0.7 copy-start.4
Sparse Core Ops, SparseCore 0:
  10.8 43.2 all-gather.1
  107.9 177.6 all-reduce.2
